TPU v7x, 32 devices: a whole 2x2x4 slice. The times are simulated.
32 devices in a mesh: tick: 16 (over z, y, x), wire: 2 (over core).
Axes of the slice: x: 2, y: 2, z: 4, core: 2. Of those that a mesh axis runs over, the one named last changes fastest.
Arguments:
- trigger: bfloat16 [2048, 16, 1280], P('tick', None, 'wire'), may hold values from -6 to 6
- response: float32 [2, 21, 1024], replicated, may hold values from -1.2 to 1.2
- wiener: float32 [1024], replicated, may hold values from 0.2 to 2
- roi_mask: int32 [16, 1280, 16], P('tick', 'wire'), may hold values 0 or 1
- cell_map: int32 [16, 1280], P('tick', 'wire'), may hold values from 0 to 127, as said below
Outputs:
- signal: bfloat16 [16, 1280, 2048], P('tick', 'wire')
- cell_charge: float32 [128, 2048], P('tick', 'wire')
Inputs may be any that keep to these rules, and one draw needn't show every extreme that they name: `cell_map`: A channel's cell c belongs to owner c // 8. Among the 640 channels of one device (an aligned block of 640 wires of one plane), at most 80 name cells of one owner; in every draw some owner gets exactly 80 channels from every such block.
All inputs are finite; a program needn't handle non-finite values. No bound on the sum of `roi_mask` on one device may be relied on, other than what follows from the above.
Results may differ from a plain program's by a relative error of at most 0.008.
Values may be sent and summed in bfloat16 or wider, within the bound.
A program may use at most 128 MiB of HBM per device.

v0:
```python
import math

import jax
import jax.numpy as jnp
from jax import lax
from jax.sharding import PartitionSpec as P

TICKS = 2048
RESP_TAPS = 21
ROI_TICKS = 128
CELLS_OWN = 8
FREQS = 1024
HALO = 10


charge_scale = 0.1


def with_halo(cells, sides, width):
    for axis, dim in sides:
        count = lax.axis_size(axis)
        ends = count - 1
        head = lax.slice_in_dim(cells, 0, width, axis=dim)
        tail = lax.slice_in_dim(cells, cells.shape[dim] - width, cells.shape[dim], axis=dim)
        cells = jnp.concatenate(
            [
                lax.ppermute(tail, axis, [(i, (i + 1) % count) for i in range(ends)]),
                cells,
                lax.ppermute(head, axis, [((i + 1) % count, i) for i in range(ends)]),
            ],
            axis=dim,
        )
    return cells


def build_tables():
    frequency = jnp.arange(FREQS, dtype=jnp.int32)
    tick_index = jnp.arange(TICKS, dtype=jnp.int32)
    phase_angle = (frequency[:, None] * tick_index[None, :] % TICKS).astype(jnp.float32) * (
        2.0 * math.pi / TICKS
    )
    cosine = jnp.cos(phase_angle).astype(jnp.bfloat16)
    sine_table = jnp.sin(phase_angle).astype(jnp.bfloat16)
    forward = jnp.concatenate([cosine, -sine_table], axis=0)
    weight = jnp.where(frequency == 0, 1.0, 2.0).astype(jnp.bfloat16)[:, None]
    inverse = jnp.concatenate([cosine * weight, -sine_table * weight], axis=0)
    return (forward, inverse)


def transform(forward, waves):
    return (jnp.dot(forward, waves, preferred_element_type=jnp.float32) * TICKS ** (-0.5)).astype(
        jnp.bfloat16
    )


def deconvolve(spectrum, response, wiener, wire_count):
    real_part = spectrum[:FREQS].astype(jnp.float32)
    imag_part = spectrum[FREQS:].astype(jnp.float32)
    sum_real = jnp.zeros((FREQS, wire_count), jnp.float32)
    sum_imag = jnp.zeros((FREQS, wire_count), jnp.float32)
    for offset in range(RESP_TAPS):
        shifted_real = real_part[:, offset : offset + wire_count]
        shifted_imag = imag_part[:, offset : offset + wire_count]
        resp_real = response[0, offset][:, None]
        resp_imag = response[1, offset][:, None]
        sum_real = sum_real + resp_real * shifted_real - resp_imag * shifted_imag
        sum_imag = sum_imag + resp_real * shifted_imag + resp_imag * shifted_real
    gain_column = wiener[:, None]
    return jnp.concatenate([sum_real * gain_column, sum_imag * gain_column], axis=0).astype(
        jnp.bfloat16
    )


def on_device(trigger, response, wiener, roi_mask, cell_map):
    forward, inverse = build_tables()
    wire_count = trigger.shape[2]
    norm_factor = TICKS ** (-0.5)
    local_spectrum = transform(
        forward, lax.all_to_all(trigger, "tick", split_axis=1, concat_axis=0, tiled=True)[:, 0, :]
    )
    spectrum = with_halo(local_spectrum, (("wire", 1),), HALO)
    filtered = deconvolve(spectrum, response, wiener, wire_count)
    unmasked = (
        lax.dot_general(
            filtered, inverse, (((0,), (0,)), ((), ())), preferred_element_type=jnp.float32
        )
        * norm_factor
    )
    blocks = roi_mask[0].astype(jnp.float32)
    signal = (
        (unmasked.reshape(wire_count, -1, ROI_TICKS) * blocks[:, :, None])
        .reshape(wire_count, TICKS)
        .astype(jnp.bfloat16)
    )
    channel_cells = cell_map[0]
    labels = jnp.arange(CELLS_OWN * lax.axis_size("tick"), dtype=jnp.int32)
    selector = (channel_cells[None, :] == labels[:, None]).astype(jnp.bfloat16)
    partial_value = lax.psum_scatter(
        jnp.dot(selector, signal, preferred_element_type=jnp.float32),
        "tick",
        scatter_dimension=0,
        tiled=True,
    )
    halves = lax.psum_scatter(
        partial_value.astype(jnp.bfloat16), "wire", scatter_dimension=1, tiled=True
    ).astype(jnp.float32)
    return (signal[None], halves * charge_scale)


def solution(mesh):
    in_specs = (P("tick", None, "wire"), P(), P(), P("tick", "wire", None), P("tick", "wire"))
    out_specs = (P("tick", "wire", None), P("tick", "wire"))
    return jax.shard_map(
        on_device, mesh=mesh, in_specs=in_specs, out_specs=out_specs, check_vma=False
    )
```

profile of v0, /device:TPU:0, one launch (start us, length us, event | category | flops | bytes accessed | tf_op | source)
XLA Modules:
  0.0 273.0 jit_solution(17339042890176495829)
XLA Ops:
  7.2 3.8 %copy.8 = bf16[128,16,640]{2,0,1:T(8,128)(2,1)} copy(bf16[128,16,640]{2,1,0:T(8,128)(2,1)} %param.5) | data formatting | bytes 5242880 | tf_op args[0]
  11.0 8.5 %all-to-all-start = ((bf16[128,16,640]{2,0,1:T(8,128)(2,1)}), bf16[128,16,640]{2,0,1:T(8,128)(2,1)}, u32[]{:S(2)}, u32[]{:S(2)}) async-start(bf16[128,16,640]{2,0,1:T(8,128)(2,1)} %copy.8), calls=%async_computation | async-start | bytes 5242880 | tf_op jit(solution)/shard_map/all_to_all | solution.py:79
  19.5 0.0 reduce-scatter.3.cloned.1.call-start
  19.6 0.1 fusion.28
  19.6 0.1 fusion.29
  19.7 31.4 %cosine_convert_fusion = bf16[1024,2048]{1,0:T(8,128)(2,1)} fusion(), kind=kLoop, calls=%fused_computation.15 | loop fusion | flops 31457280 | bytes 4194304 | tf_op jit(solution)/shard_map/convert_element_type | solution.py:42
  51.1 32.0 %fusion.15 = bf16[1024,2048]{1,0:T(8,128)(2,1)} fusion(), kind=kLoop, calls=%fused_computation.22 | loop fusion | flops 37748736 | bytes 4194304 | tf_op jit(solution)/shard_map/neg | solution.py:44
  83.2 35.4 %broadcast_multiply_fusion.1 = (bf16[1024,2048]{1,0:T(8,128)(2,1)}, bf16[1024,2048]{1,0:T(8,128)(2,1)}) fusion(bf16[1024]{0:T(1024)(128)(2,1)S(1)} %select_convert_fusion), kind=kLoop, calls=%fused_computation.30 | loop fusion | flops 50331648 | bytes 8390656 | tf_op jit(solution)/shard_map/mul | solution.py:46
  118.5 0.0 copy-start.6
  118.5 9.9 %multiply_convert_fusion = bf16[2048,640]{0,1:T(8,128)(2,1)S(1)} fusion(bf16[2048,640]{1,0:T(8,128)(2,1)} %bitcast.3, bf16[1024,2048]{1,0:T(8,128)(2,1)} %fusion.15, bf16[1024,2048]{1,0:T(8,128)(2,1)} %cosine_convert_fusion), kind=kOutput, calls=%fused_computation.21 | convolution fusion | flops 5388107776 | bytes 13631488 | tf_op jit(solution)/shard_map/dot_general | solution.py:51
  128.4 1.5 collective-permute-start
  129.9 1.5 collective-permute-start.1
  131.4 0.2 copy.9
  131.6 1.4 collective-permute-done.1
  133.1 0.7 pad_maximum_fusion
  133.8 0.0 copy-start.5
  133.8 0.7 slice_convert_fusion.1
  134.5 15.2 %multiply_convert_fusion.2 = bf16[1024,640]{0,1:T(8,128)(2,1)} fusion(f32[1024,660]{0,1:T(8,128)S(1)} %get-tuple-element.3, f32[1024,660]{0,1:T(8,128)S(1)} %get-tuple-element.2, f32[1024]{0:T(1024)S(1)} %copy-done.5, f32[1024]{0:T(1024)S(1)} %bitcast.139, f32[1024]{0:T(1024)S(1)} %bitcast.141, f32[1024]{0:T(1024)S(1)} %bitcast.61, f32[1024]{0:T(1024)S(1)} %bitcast.63, ...), kind=kLoop, calls=%fused_computation.28 | loop fusion | flops 55705600 | bytes 111587328 | tf_op jit(solution)/shard_map/convert
  149.7 15.1 %multiply_convert_fusion.1 = bf16[1024,640]{0,1:T(8,128)(2,1)} fusion(f32[1024,660]{0,1:T(8,128)S(1)} %get-tuple-element.3, f32[1024,660]{0,1:T(8,128)S(1)} %get-tuple-element.2, f32[1024]{0:T(1024)S(1)} %copy-done.5, f32[1024]{0:T(1024)S(1)} %bitcast.140, f32[1024]{0:T(1024)S(1)} %bitcast.142, f32[1024]{0:T(1024)S(1)} %bitcast.62, f32[1024]{0:T(1024)S(1)} %bitcast.64, ...), kind=kLoop, calls=%fused_computation.27 | loop fusion | flops 55705600 | bytes 111587328 | tf_op jit(solution)/shard_map/convert.1
  164.8 1.5 mul.957
  166.3 0.7 copy-done
  167.0 0.4 copy-done.2
  167.4 9.8 %fusion.14 = bf16[640,2048]{1,0:T(8,128)(2,1)S(1)} fusion(f32[80,8,16,128]{3,2,1,0:T(8,128)S(1)} %bitcast.57, bf16[1024,2048]{1,0:T(8,128)(2,1)} %get-tuple-element.49, bf16[1024,2048]{1,0:T(8,128)(2,1)S(1)} %copy-done, bf16[1024,640]{0,1:T(8,128)(2,1)} %multiply_convert_fusion.1, bf16[1024,640]{0,1:T(8,128)(2,1)S(1)} %copy-done.2), kind=kOutput, calls=%fused_computation.20 | convolution fusion | flops 5394661376 | bytes 18874368 | tf_op jit(solution)/shard_map/dot_general | solution.py:84
  177.2 0.0 copy-start.1
  177.2 1.8 fusion.23
  179.1 0.0 reduce-scatter.3.cloned.1.call-update
  179.1 0.0 reduce-scatter.5.cloned.1.call-start
  179.2 78.9 %reduce-scatter.3.cloned.1.call-done = f32[8,2048]{1,0:T(8,128)} async-done(((f32[128,2048]{1,0:T(8,128)}), f32[8,2048]{1,0:T(8,128)}) %reduce-scatter.3.cloned.1.call-update) | async-done | bytes 65552 | tf_op jit(solution)/shard_map/reduce_scatter | solution.py:98
  258.0 1.5 convert_element_type.68
  259.5 0.0 reduce-scatter.5.cloned.1.call-update
  259.5 5.3 %reduce-scatter.5.cloned.1.call-done = bf16[8,1024]{1,0:T(8,128)(2,1)} async-done(((bf16[8,2048]{1,0:T(8,128)(2,1)}), bf16[8,1024]{1,0:T(8,128)(2,1)}) %reduce-scatter.5.cloned.1.call-update) | async-done | bytes 16400 | tf_op jit(solution)/shard_map/reduce_scatter | solution.py:104
  264.8 1.3 convert_multiply_fusion
  (16 shorter events, 0.1 us)
Async XLA Ops:
  11.0 8.6 %copy-start.4 = (s32[1,640,16]{1,2,0:T(8,128)S(1)}, s32[1,640,16]{1,2,0:T(8,128)}, u32[]{:S(2)}) copy-start(s32[1,640,16]{1,2,0:T(8,128)} %param.8) | copy-start | bytes 122884
  11.0 8.6 %copy-start.3 = (f32[2,21,1024]{2,0,1:T(2,128)S(1)}, f32[2,21,1024]{2,0,1:T(2,128)}, u32[]{:S(2)}) copy-start(f32[2,21,1024]{2,0,1:T(2,128)} %param.6) | copy-start | bytes 516100
  11.0 107.5 %all-to-all-start = ((bf16[128,16,640]{2,0,1:T(8,128)(2,1)}), bf16[128,16,640]{2,0,1:T(8,128)(2,1)}, u32[]{:S(2)}, u32[]{:S(2)}) async-start(bf16[128,16,640]{2,0,1:T(8,128)(2,1)} %copy.8), calls=%async_computation | async-start | bytes 5242880 | tf_op jit(solution)/shard_map/all_to_all | solution.py:79
  19.5 238.5 %reduce-scatter.3.cloned.1.call-start = ((), (), s32[]{:S(2)}) async-start(), calls=%async_computation.3 | async-start | bytes 1114112 | tf_op jit(solution)/shard_map/reduce_scatter | solution.py:98
  118.5 13.1 %copy-start.6 = (s32[1,640]{1,0:T(1,128)S(1)}, s32[1,640]{1,0:T(1,128)}, u32[]{:S(2)}) copy-start(s32[1,640]{1,0:T(1,128)} %param.9) | copy-start | bytes 7684
  128.4 3.2 %collective-permute-start = (bf16[2048,10]{0,1:T(8,128)(2,1)S(1)}, bf16[2048,10]{0,1:T(8,128)(2,1)S(1)}, u32[]{:S(2)}, u32[]{:S(2)}) collective-permute-start(bf16[2048,10]{0,1:T(8,128)(2,1)S(1)} %get-tuple-element.4), channel_id=1, source_target_pairs={{0,1},{2,3},{4,5},{6,7},{8,9},{10,11},{12,13},{14,15},{16,17},{18,... | collective-permute-start | bytes 122888 | tf_op jit(solution)/shard_map/ppermute | solution.py:27
  129.9 3.1 %collective-permute-start.1 = (bf16[2048,10]{0,1:T(8,128)(2,1)S(1)}, bf16[2048,10]{0,1:T(8,128)(2,1)S(1)}, u32[]{:S(2)}, u32[]{:S(2)}) collective-permute-start(bf16[2048,10]{0,1:T(8,128)(2,1)S(1)} %get-tuple-element.5), channel_id=1, source_target_pairs={{1,0},{3,2},{5,4},{7,6},{9,8},{11,10},{13,12},{15,14},{17,16},{19,... | collective-permute-start | bytes 122888 | tf_op jit(solution)/shard_map/ppermute | solution.py:29
  133.8 0.7 copy-start.5
  164.8 2.2 copy-start
  164.8 2.6 copy-start.2
  177.2 88.9 %copy-start.1 = (bf16[640,2048]{1,0:T(8,128)(2,1)}, bf16[640,2048]{1,0:T(8,128)(2,1)S(1)}, u32[]{:S(2)}) copy-start(bf16[640,2048]{1,0:T(8,128)(2,1)S(1)} %fusion.14) | copy-start | bytes 7864324
  179.1 85.7 %reduce-scatter.5.cloned.1.call-start = ((), (), s32[]{:S(2)}) async-start(), calls=%async_computation.4 | async-start | bytes 49152 | tf_op jit(solution)/shard_map/reduce_scatter | solution.py:104
Sparse Core Ops, SparseCore 0:
  179.2 78.7 reduce-scatter.2
  260.9 3.9 reduce-scatter.4
where the time goes:
time: 273 us
  other arithmetic  133 us (49%)
  waiting for transfers between devices  85.6 us (31%)
  matrix products  21.6 us (8%)
  between operations  14.2 us (5%)
  starting transfers between devices  11.5 us (4%)
  local copies, waits for them, and re-layouts  6.73 us (2%)
    reduce_scatter x1, waiting for transfers between devices, on_device(): lax.psum_scatter(jnp.dot(selector, signal, preferred_element_type=jnp.flo...  78.9 us
    mul x1, other arithmetic, build_tables(): inverse = jnp.concatenate([cosine * weight, -sine_table * weight], axis=0)  35.4 us
    neg x1, other arithmetic, build_tables(): forward = jnp.concatenate([cosine, -sine_table], axis=0)  32 us
    convert_element_type x1, other arithmetic, build_tables(): cosine = jnp.cos(phase_angle).astype(jnp.bfloat16)  31.4 us
    another operation x2, other arithmetic  30.3 us
    dot_general x1, matrix products, transform(): jnp.dot(forward, waves, preferred_element_type=jnp.float32)  9.88 us
    dot_general x1, matrix products, on_device(): lax.dot_general(filtered, inverse, (((0,), (0,)), ((), ())), preferred_el...  9.84 us
    all_to_all x1, starting transfers between devices, on_device(): lax.all_to_all(trigger, 'tick', split_axis=1, concat_axis=0, tiled=True)  8.49 us
  transfers between devices with their start and end apart: 5, of which 3 were waited for; matrix products, arithmetic and copies ran while one was open for 36% of the time, Pallas kernels for 0%

commit v1 on v0

v1 whole, which is shorter than its diff:
```python
import functools
import math

import jax
import jax.numpy as jnp
import ml_dtypes
import numpy as np
from jax import lax
from jax.experimental import pallas as pl
from jax.experimental.pallas import tpu as pltpu
from jax.sharding import PartitionSpec as P

TICKS = 2048
RESP_TAPS = 21
ROI_TICKS = 128
CELLS_OWN = 8
FREQS = 1024
HALO = 10
PAD = 16
LANES = 128
FTILES = FREQS // LANES
CHARGE_SCALE = 0.1
MESH = pl.DeviceIdType.MESH
CHUNKS = (256, 256, 128)
ROWS = 16


def build_table():
    frequency = np.arange(FREQS, dtype=np.int64)
    tick = np.arange(TICKS, dtype=np.int64)
    angle = ((tick[:, None] * frequency[None, :]) % TICKS).astype(np.float32) * np.float32(
        2.0 * math.pi / TICKS
    )
    cosine = np.cos(angle).astype(ml_dtypes.bfloat16).reshape(TICKS, FTILES, LANES)
    sine = (-np.sin(angle)).astype(ml_dtypes.bfloat16).reshape(TICKS, FTILES, LANES)
    return np.concatenate([cosine, sine], axis=2).reshape(TICKS, 2 * FREQS)


def windows(wires):
    chunks, outs, start = [], [], 0
    done = 0
    for size in CHUNKS:
        stop = start + size
        chunks.append((start, size))
        last = wires if stop == wires else stop - PAD
        outs.append((done, last - done))
        start, done = stop, last
    return chunks, outs


def kernel(
    n,
    x_ref,
    table_hbm,
    response_ref,
    wiener_ref,
    mask_ref,
    cells_ref,
    signal_ref,
    charge_ref,
    table,
    waves,
    turned,
    spec,
    coef,
    filtered,
    signal,
    selector,
    pair_out,
    pair_in,
    own_part,
    cell_out,
    cell_in,
    send_sem,
    recv_sem,
    local_sem,
    table_sem,
    halo_sem,
    pair_sem,
    cell_sem,
    out_sem,
):
    me = lax.axis_index("tick")
    side = lax.axis_index("wire")
    block, wires = x_ref.shape[1], x_ref.shape[2]
    cells = CELLS_OWN * n
    half = TICKS // 2
    chunks, outs = windows(wires)

    def place(start, size, unit):
        return pl.multiple_of(jnp.where(side == 1, start, wires - start - size), unit)

    table_copy = pltpu.make_async_copy(table_hbm, table, table_sem)
    table_copy.start()

    barrier = pltpu.get_barrier_semaphore()

    @pl.loop(1, n)
    def _(k):
        pl.semaphore_signal(
            barrier, inc=1, device_id={"tick": lax.rem(me + k, n)}, device_id_type=MESH
        )

    pl.semaphore_signal(barrier, inc=1, device_id={"wire": 1 - side}, device_id_type=MESH)
    pl.semaphore_wait(barrier, n)

    mine = pl.ds(pl.multiple_of(me * block, block), block)
    for c, (start, size) in enumerate(chunks):
        lanes = pl.ds(place(start, size, LANES), size)

        @pl.loop(1, n)
        def _(k):
            peer = lax.rem(me + k, n)
            pltpu.make_async_remote_copy(
                src_ref=x_ref.at[peer, :, lanes],
                dst_ref=waves.at[mine, lanes],
                send_sem=send_sem.at[c],
                recv_sem=recv_sem.at[c],
                device_id={"tick": peer},
                device_id_type=MESH,
            ).start()

    local_copy = pltpu.make_async_copy(x_ref.at[me], waves.at[mine, :], local_sem)
    local_copy.start()

    for j in range(FTILES):
        cols = slice(j * LANES, (j + 1) * LANES)
        gain = wiener_ref[:, cols] * (2.0 / TICKS)
        if j == 0:
            gain = jnp.where(lax.broadcasted_iota(jnp.int32, (1, LANES), 1) == 0, 0.5, 1.0) * gain
        real = response_ref[0, :, cols] * gain
        imag = response_ref[1, :, cols] * gain
        coef[j, 0, 0:RESP_TAPS, :] = real
        coef[j, 1, 0:RESP_TAPS, :] = real + imag
        coef[j, 2, 0:RESP_TAPS, :] = imag - real

    labels = lax.broadcasted_iota(jnp.int32, (cells, wires), 0)
    selector[...] = (cells_ref[...] == labels).astype(jnp.float32).astype(jnp.bfloat16)
    outer = pl.multiple_of(jnp.where(side == 1, PAD + wires, 0), PAD)
    for part in range(3):
        spec[part, :, pl.ds(outer, PAD), :] = jnp.zeros((FTILES, PAD, LANES), jnp.float32)

    def halo_copy():
        src = pl.multiple_of(jnp.where(side == 1, PAD, wires), PAD)
        dst = pl.multiple_of(jnp.where(side == 1, PAD + wires, 0), PAD)
        return pltpu.make_async_remote_copy(
            src_ref=spec.at[:, :, pl.ds(src, PAD), :],
            dst_ref=spec.at[:, :, pl.ds(dst, PAD), :],
            send_sem=halo_sem.at[0],
            recv_sem=halo_sem.at[1],
            device_id={"wire": 1 - side},
            device_id_type=MESH,
        )

    local_copy.wait()
    table_copy.wait()
    out_copies = []
    for c, ((start, size), (first, count)) in enumerate(zip(chunks, outs)):
        base = place(start, size, LANES)
        lanes = pl.ds(base, size)
        others = waves.at[pl.ds(0, (n - 1) * block), lanes]
        pltpu.make_async_copy(others, others, recv_sem.at[c]).wait()
        turned[0:size, :] = waves[:, lanes].T

        @pl.loop(0, FTILES)
        def _(j):
            cols = pl.ds(pl.multiple_of(j * 2 * LANES, 2 * LANES), 2 * LANES)
            product = jnp.dot(
                turned[0:size, :], table[:, cols], preferred_element_type=jnp.float32
            )
            real, imag = product[:, :LANES], product[:, LANES:]
            rows = pl.ds(pl.multiple_of(base + PAD, PAD), size)
            spec[0, j, rows, :] = real
            spec[1, j, rows, :] = imag
            spec[2, j, rows, :] = real + imag

        if c == 0:
            halo = halo_copy()
            halo.start()
            halo.wait()

        at = place(first, count, PAD)

        @pl.loop(0, FTILES)
        def _(j):
            @pl.loop(0, count // ROWS)
            def _(b):
                row = pl.multiple_of(at + b * ROWS, ROWS)
                acc_s = jnp.zeros((ROWS, LANES), jnp.float32)
                acc_i = jnp.zeros((ROWS, LANES), jnp.float32)
                acc_r = jnp.zeros((ROWS, LANES), jnp.float32)
                for d in range(RESP_TAPS):
                    rows = pl.ds(row + (PAD - HALO + d), ROWS)
                    acc_s = acc_s + coef[j, 0, d : d + 1, :] * spec[2, j, rows, :]
                    acc_i = acc_i + coef[j, 1, d : d + 1, :] * spec[1, j, rows, :]
                    acc_r = acc_r + coef[j, 2, d : d + 1, :] * spec[0, j, rows, :]
                col = pl.multiple_of(j * 2 * LANES, 2 * LANES)
                both = jnp.concatenate([acc_s - acc_i, acc_s + acc_r], axis=1)
                filtered[pl.ds(row, ROWS), pl.ds(col, 2 * LANES)] = both.astype(jnp.bfloat16)

        out_rows = pl.ds(at, count)
        roi = mask_ref[out_rows, :].astype(jnp.float32).astype(jnp.bfloat16)

        @pl.loop(0, TICKS // 256)
        def _(i):
            ticks = pl.ds(pl.multiple_of(i * 256, 256), 256)
            unmasked = lax.dot_general(
                filtered[out_rows, :],
                table[ticks, :],
                (((1,), (1,)), ((), ())),
                preferred_element_type=jnp.float32,
            )
            shape = (TICKS // ROI_TICKS, 256)
            spread = (
                lax.broadcasted_iota(jnp.int32, shape, 1) // ROI_TICKS + i * (256 // ROI_TICKS)
                == lax.broadcasted_iota(jnp.int32, shape, 0)
            ).astype(jnp.float32).astype(jnp.bfloat16)
            keep = jnp.dot(roi, spread, preferred_element_type=jnp.float32)
            signal[out_rows, ticks] = (unmasked * keep).astype(jnp.bfloat16)

        out_copy = pltpu.make_async_copy(
            signal.at[out_rows, :], signal_ref.at[out_rows, :], out_sem.at[c]
        )
        out_copy.start()
        out_copies.append(out_copy)

    def charge_of(which):
        lanes = pl.ds(pl.multiple_of(which * half, half), half)
        return jnp.dot(selector[...], signal[:, lanes], preferred_element_type=jnp.float32)

    pair_out[...] = charge_of(1 - side).astype(jnp.bfloat16)
    pair_copy = pltpu.make_async_remote_copy(
        src_ref=pair_out,
        dst_ref=pair_in,
        send_sem=pair_sem.at[0],
        recv_sem=pair_sem.at[1],
        device_id={"wire": 1 - side},
        device_id_type=MESH,
    )
    pair_copy.start()
    own_part[...] = charge_of(side)
    pair_copy.wait()
    quarter = half // 2

    total = (own_part[...] + pair_in[...].astype(jnp.float32)).reshape(n, CELLS_OWN, half)
    cell_out[...] = jnp.concatenate(
        [total[:, :, :quarter], total[:, :, quarter:]], axis=1
    ).astype(jnp.bfloat16)

    @pl.loop(1, n)
    def _(k):
        peer = lax.rem(me + k, n)
        pltpu.make_async_remote_copy(
            src_ref=cell_out.at[peer],
            dst_ref=cell_in.at[me],
            send_sem=cell_sem.at[0],
            recv_sem=cell_sem.at[1],
            device_id={"tick": peer},
            device_id_type=MESH,
        ).start()

    own_copy = pltpu.make_async_copy(cell_out.at[me], cell_in.at[me], local_sem)
    own_copy.start()
    own_copy.wait()
    arrived = cell_in.at[pl.ds(0, n - 1)]
    pltpu.make_async_copy(arrived, arrived, cell_sem.at[1]).wait()
    summed = jnp.sum(cell_in[...].astype(jnp.float32), axis=0) * CHARGE_SCALE
    charge_ref[:, 0:quarter] = summed[:CELLS_OWN]
    charge_ref[:, quarter:half] = summed[CELLS_OWN:]

    sent = cell_out.at[pl.ds(0, n - 1)]
    pltpu.make_async_copy(sent, sent, cell_sem.at[0]).wait()
    for c, (start, size) in enumerate(chunks):
        others = waves.at[pl.ds(0, (n - 1) * block), pl.ds(place(start, size, LANES), size)]
        pltpu.make_async_copy(others, others, send_sem.at[c]).wait()
    for out_copy in out_copies:
        out_copy.wait()


def on_device(trigger, response, wiener, roi_mask, cell_map):
    n = lax.axis_size("tick")
    wires = trigger.shape[2]
    cells = CELLS_OWN * n
    table = jnp.asarray(build_table())
    x = jnp.swapaxes(trigger, 0, 1)
    any_space = pl.BlockSpec(memory_space=pl.ANY)
    vmem = pl.BlockSpec(memory_space=pltpu.VMEM)
    bf16, f32 = jnp.bfloat16, jnp.float32
    half = TICKS // 2
    dma = pltpu.SemaphoreType.DMA
    signal, charge = pl.pallas_call(
        functools.partial(kernel, n),
        out_shape=(
            jax.ShapeDtypeStruct((wires, TICKS), bf16),
            jax.ShapeDtypeStruct((CELLS_OWN, half), f32),
        ),
        in_specs=[any_space, any_space, vmem, vmem, vmem, vmem],
        out_specs=(any_space, vmem),
        scratch_shapes=[
            pltpu.VMEM((TICKS, 2 * FREQS), bf16),
            pltpu.VMEM((TICKS, wires), bf16),
            pltpu.VMEM((max(CHUNKS), TICKS), bf16),
            pltpu.VMEM((3, FTILES, wires + 2 * PAD, LANES), f32),
            pltpu.VMEM((FTILES, 3, 24, LANES), f32),
            pltpu.VMEM((wires, 2 * FREQS), bf16),
            pltpu.VMEM((wires, TICKS), bf16),
            pltpu.VMEM((cells, wires), bf16),
            pltpu.VMEM((cells, half), bf16),
            pltpu.VMEM((cells, half), bf16),
            pltpu.VMEM((cells, half), f32),
            pltpu.VMEM((n, 16, half // 2), bf16),
            pltpu.VMEM((n, 16, half // 2), bf16),
            dma((len(CHUNKS),)),
            dma((len(CHUNKS),)),
            dma,
            dma,
            dma((2,)),
            dma((2,)),
            dma((2,)),
            dma((len(CHUNKS),)),
        ],
        compiler_params=pltpu.CompilerParams(
            collective_id=0, has_side_effects=True, vmem_limit_bytes=56 * 1024 * 1024
        ),
        cost_estimate=pl.CostEstimate(
            flops=4 * wires * TICKS * 2 * FREQS, bytes_accessed=20_000_000, transcendentals=0
        ),
    )(x, table, response, wiener[None], roi_mask[0], cell_map)
    return (signal[None], charge)


def solution(mesh):
    in_specs = (P("tick", None, "wire"), P(), P(), P("tick", "wire", None), P("tick", "wire"))
    out_specs = (P("tick", "wire", None), P("tick", "wire"))
    return jax.shard_map(
        on_device, mesh=mesh, in_specs=in_specs, out_specs=out_specs, check_vma=False
    )
```

time: 273 us -> 111 us (0.41)
  other arithmetic: 133 us -> 0 us
  Pallas kernels: 0 us -> 98.8 us
  waiting for transfers between devices: 85.6 us -> 0 us
  matrix products: 21.6 us -> 0 us
  between operations: 14.2 us -> 0.65 us
  starting transfers between devices: 11.5 us -> 0 us
  local copies, waits for them, and re-layouts: 6.73 us -> 11.3 us
    pallas_call x0 -> x1, Pallas kernels: none -> 98.8 us  [on_device(): pl.pallas_call(functools.partial(kernel, n), out_shape=(jax.ShapeDtypeStr...]
    reduce_scatter x2 -> x0, waiting for transfers between devices: 84.2 us -> none  [the longest x1 78.9 us: on_device(): lax.psum_scatter(jnp.dot(selector, signal, preferred_element_type=jnp.flo...]
    mul x2 -> x0, other arithmetic: 36.7 us -> none  [the longest x1 35.4 us: build_tables(): inverse = jnp.concatenate([cosine * weight, -sine_table * weight], axis=0)]
    convert_element_type x5 -> x0, other arithmetic: 33.6 us -> none  [the longest x1 31.4 us: build_tables(): cosine = jnp.cos(phase_angle).astype(jnp.bfloat16)]
    neg x1 -> x0, other arithmetic: 32 us -> none  [build_tables(): forward = jnp.concatenate([cosine, -sine_table], axis=0)]
    another operation x2 -> x0, other arithmetic: 30.3 us -> none
    dot_general x3 -> x0, matrix products: 21.6 us -> none  [the longest x1 9.88 us: transform(): jnp.dot(forward, waves, preferred_element_type=jnp.float32)]
    all_to_all x1 -> x0, starting transfers between devices: 8.49 us -> none  [on_device(): lax.all_to_all(trigger, 'tick', split_axis=1, concat_axis=0, tiled=True)]
  transfers between devices with their start and end apart: 5 -> 0, of which waited for: 3 -> 0; matrix products, arithmetic and copies ran while one was open for 36% -> 0% of each run, Pallas kernels for 0% -> 0%
where the time goes in v1:
time: 111 us
  Pallas kernels  98.8 us (89%)
  local copies, waits for them, and re-layouts  11.3 us (10%)
    pallas_call x1, Pallas kernels, on_device(): pl.pallas_call(functools.partial(kernel, n), out_shape=(jax.ShapeDtypeStr...  98.8 us
    unnamed x7, local copies, waits for them, and re-layouts  11.3 us

profile of v1, /device:TPU:0, one launch (start us, length us, event | category | flops | bytes accessed | tf_op | source)
XLA Modules:
  0.0 110.8 jit_solution(13800941208307863101)
XLA Ops:
  0.6 1.7 %copy.10.response_ref = f32[2,21,1024]{2,1,0:T(8,128)} copy(f32[2,21,1024]{2,0,1:T(2,128)} %param.7) | data formatting | bytes 344064 | tf_op args[1]
  2.3 1.7 %copy.9 = s32[1,640,16]{2,1,0:T(8,128)} copy(s32[1,640,16]{1,2,0:T(8,128)} %param.9) | data formatting | bytes 81920 | tf_op args[3]
  4.0 3.8 %copy.12 = bf16[128,16,640]{2,0,1:T(8,128)(2,1)} copy(bf16[128,16,640]{2,1,0:T(8,128)(2,1)} %param.6) | data formatting | bytes 5242880 | tf_op args[0]
  7.8 98.8 %shard_map.77 = (bf16[640,2048]{1,0:T(8,128)(2,1)}, f32[8,1024]{1,0:T(8,128)}) custom-call(bf16[16,128,640]{2,1,0:T(8,128)(2,1)} %bitcast.7, bf16[2048,2048]{1,0:T(8,128)(2,1)} %constant.2.clone.table_hbm, f32[2,21,1024]{2,1,0:T(8,128)} %copy.10.response_ref, f32[1,1024]{1,0:T(1,128)} %bitcast.9, s32[640,16]{1,0:T(8,128)} %bitcast.8, s32[1,640]{1,0:T(1,128)} %cells_ref.1), custom_call_target="tpu_custom_call" | custom-call | flops 10737418240 | bytes 20000000 | tf_op jit(solution)/shard_map/pallas_call | solution.py:291
  106.6 0.0 copy-start
  106.7 3.6 %copy.15 = bf16[1,640,2048]{2,1,0:T(8,128)(2,1)} copy(bf16[1,640,2048]{2,1,0:T(8,128)(2,1)} %bitcast.6) | data formatting | bytes 5242880
  110.2 0.0 copy-done
  110.2 0.6 copy.16
Async XLA Ops:
  106.6 3.6 %copy-start = (f32[8,1024]{1,0:T(8,128)S(1)}, f32[8,1024]{1,0:T(8,128)}, u32[]{:S(2)}) copy-start(f32[8,1024]{1,0:T(8,128)} %get-tuple-element.9) | copy-start | bytes 98308

commit v2 on v1

--- a/solution.py
+++ b/solution.py
@@ -21,19 +21,22 @@
 FTILES = FREQS // LANES
 CHARGE_SCALE = 0.1
 MESH = pl.DeviceIdType.MESH
-CHUNKS = (256, 256, 128)
+CHUNKS = (128, 128, 128, 128, 128)
+AHEAD = 2
 ROWS = 16
+MOVES = 5
 
 
 def build_table():
-    frequency = np.arange(FREQS, dtype=np.int64)
-    tick = np.arange(TICKS, dtype=np.int64)
-    angle = ((tick[:, None] * frequency[None, :]) % TICKS).astype(np.float32) * np.float32(
+    order = np.arange(FREQS, dtype=np.int64).reshape(FREQS // 2, 2).T.reshape(-1)
+    tick = np.arange(TICKS // 2, dtype=np.int64)
+    angle = ((tick[:, None] * order[None, :]) % TICKS).astype(np.float32) * np.float32(
         2.0 * math.pi / TICKS
     )
-    cosine = np.cos(angle).astype(ml_dtypes.bfloat16).reshape(TICKS, FTILES, LANES)
-    sine = (-np.sin(angle)).astype(ml_dtypes.bfloat16).reshape(TICKS, FTILES, LANES)
-    return np.concatenate([cosine, sine], axis=2).reshape(TICKS, 2 * FREQS)
+    shape = (TICKS // 2, FTILES, LANES)
+    cosine = np.cos(angle).astype(ml_dtypes.bfloat16).reshape(shape)
+    sine = (-np.sin(angle)).astype(ml_dtypes.bfloat16).reshape(shape)
+    return np.concatenate([cosine, sine], axis=2).reshape(TICKS // 2, 2 * FREQS)
 
 
 def windows(wires):
@@ -52,6 +55,7 @@
     n,
     x_ref,
     table_hbm,
+    back_hbm,
     response_ref,
     wiener_ref,
     mask_ref,
@@ -59,6 +63,8 @@
     signal_ref,
     charge_ref,
     table,
+    back,
+    roi,
     waves,
     turned,
     spec,
@@ -75,6 +81,7 @@
     recv_sem,
     local_sem,
     table_sem,
+    back_sem,
     halo_sem,
     pair_sem,
     cell_sem,
@@ -92,6 +99,8 @@
 
     table_copy = pltpu.make_async_copy(table_hbm, table, table_sem)
     table_copy.start()
+    back_copy = pltpu.make_async_copy(back_hbm, back, back_sem)
+    back_copy.start()
 
     barrier = pltpu.get_barrier_semaphore()
 
@@ -105,7 +114,8 @@
     pl.semaphore_wait(barrier, n)
 
     mine = pl.ds(pl.multiple_of(me * block, block), block)
-    for c, (start, size) in enumerate(chunks):
+    def send(c):
+        start, size = chunks[c]
         lanes = pl.ds(place(start, size, LANES), size)
 
         @pl.loop(1, n)
@@ -120,20 +130,32 @@
                 device_id_type=MESH,
             ).start()
 
+    for c in range(AHEAD):
+        send(c)
+
     local_copy = pltpu.make_async_copy(x_ref.at[me], waves.at[mine, :], local_sem)
     local_copy.start()
 
-    for j in range(FTILES):
-        cols = slice(j * LANES, (j + 1) * LANES)
-        gain = wiener_ref[:, cols] * (2.0 / TICKS)
-        if j == 0:
-            gain = jnp.where(lax.broadcasted_iota(jnp.int32, (1, LANES), 1) == 0, 0.5, 1.0) * gain
-        real = response_ref[0, :, cols] * gain
-        imag = response_ref[1, :, cols] * gain
-        coef[j, 0, 0:RESP_TAPS, :] = real
-        coef[j, 1, 0:RESP_TAPS, :] = real + imag
-        coef[j, 2, 0:RESP_TAPS, :] = imag - real
-
+    first_one = lax.broadcasted_iota(jnp.int32, (1, FREQS), 1) == 0
+    gain = jnp.where(first_one, 0.5, 1.0) * wiener_ref[...] * (2.0 / TICKS)
+    real = response_ref[:, 0, :] * gain
+    imag = response_ref[:, 1, :] * gain
+
+    @pl.loop(0, FTILES)
+    def _(j):
+        shape = (FREQS, LANES)
+        column = lax.broadcasted_iota(jnp.int32, shape, 1) + lax.rem(j, FTILES // 2) * LANES
+        wanted = 2 * column + j // (FTILES // 2)
+        pick = (lax.broadcasted_iota(jnp.int32, shape, 0) == wanted).astype(jnp.float32)
+        picked = functools.partial(
+            jnp.dot, preferred_element_type=jnp.float32, precision=lax.Precision.HIGHEST
+        )
+        real_j, imag_j = picked(real, pick), picked(imag, pick)
+        coef[j, 0, 0:RESP_TAPS, :] = real_j
+        coef[j, 1, 0:RESP_TAPS, :] = real_j + imag_j
+        coef[j, 2, 0:RESP_TAPS, :] = imag_j - real_j
+
+    roi[...] = mask_ref[...].astype(jnp.float32).T
     labels = lax.broadcasted_iota(jnp.int32, (cells, wires), 0)
     selector[...] = (cells_ref[...] == labels).astype(jnp.float32).astype(jnp.bfloat16)
     outer = pl.multiple_of(jnp.where(side == 1, PAD + wires, 0), PAD)
@@ -154,19 +176,24 @@
 
     local_copy.wait()
     table_copy.wait()
+    back_copy.wait()
     out_copies = []
     for c, ((start, size), (first, count)) in enumerate(zip(chunks, outs)):
         base = place(start, size, LANES)
         lanes = pl.ds(base, size)
         others = waves.at[pl.ds(0, (n - 1) * block), lanes]
         pltpu.make_async_copy(others, others, recv_sem.at[c]).wait()
-        turned[0:size, :] = waves[:, lanes].T
+        if c + AHEAD < len(chunks):
+            send(c + AHEAD)
+        early, late = waves[0:half, lanes], waves[half:TICKS, lanes]
+        turned[0, 0:size, :] = (early + late).T
+        turned[1, 0:size, :] = (early - late).T
 
         @pl.loop(0, FTILES)
         def _(j):
             cols = pl.ds(pl.multiple_of(j * 2 * LANES, 2 * LANES), 2 * LANES)
             product = jnp.dot(
-                turned[0:size, :], table[:, cols], preferred_element_type=jnp.float32
+                turned[j // (FTILES // 2), 0:size, :], table[:, cols], preferred_element_type=jnp.float32
             )
             real, imag = product[:, :LANES], product[:, LANES:]
             rows = pl.ds(pl.multiple_of(base + PAD, PAD), size)
@@ -199,24 +226,26 @@
                 filtered[pl.ds(row, ROWS), pl.ds(col, 2 * LANES)] = both.astype(jnp.bfloat16)
 
         out_rows = pl.ds(at, count)
-        roi = mask_ref[out_rows, :].astype(jnp.float32).astype(jnp.bfloat16)
-
-        @pl.loop(0, TICKS // 256)
-        def _(i):
-            ticks = pl.ds(pl.multiple_of(i * 256, 256), 256)
-            unmasked = lax.dot_general(
-                filtered[out_rows, :],
-                table[ticks, :],
-                (((1,), (1,)), ((), ())),
+        blocks = roi[out_rows, :]
+        for i in range(half // 256):
+            ticks = slice(i * 256, (i + 1) * 256)
+            even = jnp.dot(
+                filtered[out_rows, 0:FREQS],
+                back[0:FREQS, ticks],
                 preferred_element_type=jnp.float32,
             )
-            shape = (TICKS // ROI_TICKS, 256)
-            spread = (
-                lax.broadcasted_iota(jnp.int32, shape, 1) // ROI_TICKS + i * (256 // ROI_TICKS)
-                == lax.broadcasted_iota(jnp.int32, shape, 0)
-            ).astype(jnp.float32).astype(jnp.bfloat16)
-            keep = jnp.dot(roi, spread, preferred_element_type=jnp.float32)
-            signal[out_rows, ticks] = (unmasked * keep).astype(jnp.bfloat16)
+            odd = jnp.dot(
+                filtered[out_rows, FREQS:],
+                back[FREQS:, ticks],
+                preferred_element_type=jnp.float32,
+            )
+            for base_tick, value in ((0, even + odd), (half, even - odd)):
+                for part in range(2):
+                    tick = base_tick + i * 256 + part * ROI_TICKS
+                    at_block = tick // ROI_TICKS
+                    keep = blocks[:, at_block : at_block + 1]
+                    kept = value[:, part * ROI_TICKS : (part + 1) * ROI_TICKS] * keep
+                    signal[out_rows, tick : tick + ROI_TICKS] = kept.astype(jnp.bfloat16)
 
         out_copy = pltpu.make_async_copy(
             signal.at[out_rows, :], signal_ref.at[out_rows, :], out_sem.at[c]
@@ -277,11 +306,19 @@
         out_copy.wait()
 
 
+def hand_over(signal_in, charge_in, signal_out, charge_out):
+    signal_out[...] = signal_in[...]
+
+    @pl.when(pl.program_id(0) == 0)
+    def _():
+        charge_out[...] = charge_in[...]
+
+
 def on_device(trigger, response, wiener, roi_mask, cell_map):
     n = lax.axis_size("tick")
     wires = trigger.shape[2]
     cells = CELLS_OWN * n
-    table = jnp.asarray(build_table())
+    table_np = build_table()
     x = jnp.swapaxes(trigger, 0, 1)
     any_space = pl.BlockSpec(memory_space=pl.ANY)
     vmem = pl.BlockSpec(memory_space=pltpu.VMEM)
@@ -294,12 +331,14 @@
             jax.ShapeDtypeStruct((wires, TICKS), bf16),
             jax.ShapeDtypeStruct((CELLS_OWN, half), f32),
         ),
-        in_specs=[any_space, any_space, vmem, vmem, vmem, vmem],
+        in_specs=[any_space, any_space, any_space, vmem, vmem, vmem, vmem],
         out_specs=(any_space, vmem),
         scratch_shapes=[
-            pltpu.VMEM((TICKS, 2 * FREQS), bf16),
+            pltpu.VMEM((half, 2 * FREQS), bf16),
+            pltpu.VMEM((2 * FREQS, half), bf16),
+            pltpu.VMEM((wires, TICKS // ROI_TICKS), f32),
             pltpu.VMEM((TICKS, wires), bf16),
-            pltpu.VMEM((max(CHUNKS), TICKS), bf16),
+            pltpu.VMEM((2, max(CHUNKS), half), bf16),
             pltpu.VMEM((3, FTILES, wires + 2 * PAD, LANES), f32),
             pltpu.VMEM((FTILES, 3, 24, LANES), f32),
             pltpu.VMEM((wires, 2 * FREQS), bf16),
@@ -314,6 +353,7 @@
             dma((len(CHUNKS),)),
             dma,
             dma,
+            dma,
             dma((2,)),
             dma((2,)),
             dma((2,)),
@@ -325,7 +365,27 @@
         cost_estimate=pl.CostEstimate(
             flops=4 * wires * TICKS * 2 * FREQS, bytes_accessed=20_000_000, transcendentals=0
         ),
-    )(x, table, response, wiener[None], roi_mask[0], cell_map)
+    )(
+        x,
+        jnp.asarray(table_np),
+        jnp.asarray(np.ascontiguousarray(table_np.T)),
+        jnp.swapaxes(response, 0, 1),
+        wiener[None],
+        jnp.swapaxes(roi_mask[0], 0, 1),
+        cell_map,
+    )
+    part = pl.BlockSpec((wires // MOVES, TICKS), lambda i: (i, 0))
+    whole = pl.BlockSpec((CELLS_OWN, half), lambda i: (0, 0))
+    signal, charge = pl.pallas_call(
+        hand_over,
+        out_shape=(
+            jax.ShapeDtypeStruct(signal.shape, bf16),
+            jax.ShapeDtypeStruct(charge.shape, f32),
+        ),
+        grid=(MOVES,),
+        in_specs=[part, whole],
+        out_specs=(part, whole),
+    )(signal, charge)
     return (signal[None], charge)
 
 

time: 111 us -> 94.5 us (0.85)
  Pallas kernels: 98.8 us -> 89.8 us
  local copies, waits for them, and re-layouts: 11.3 us -> 3.82 us
    pallas_call x1, Pallas kernels: 98.8 us -> 85.1 us  [on_device(): pl.pallas_call(functools.partial(kernel, n), out_shape=(jax.ShapeDtypeStr...]
    unnamed x7 -> x1, local copies, waits for them, and re-layouts: 11.3 us -> 3.82 us
    pallas_call x0 -> x1, Pallas kernels: none -> 4.71 us  [on_device(): pl.pallas_call(hand_over, out_shape=(jax.ShapeDtypeStruct(signal.shape, b...]
where the time goes in v2:
time: 94.5 us; the launch traced here: 94.2 us
  Pallas kernels  89.8 us (95%)
  local copies, waits for them, and re-layouts  3.82 us (4%)
    pallas_call x1, Pallas kernels, on_device(): pl.pallas_call(functools.partial(kernel, n), out_shape=(jax.ShapeDtypeStr...  85.1 us
    pallas_call x1, Pallas kernels, on_device(): pl.pallas_call(hand_over, out_shape=(jax.ShapeDtypeStruct(signal.shape, b...  4.71 us
    unnamed x1, local copies, waits for them, and re-layouts  3.82 us

profile of v2, /device:TPU:0, one launch (start us, length us, event | category | flops | bytes accessed | tf_op | source)
XLA Modules:
  0.0 94.2 jit_solution(8664960323460270722)
XLA Ops:
  0.6 3.8 %copy.11 = bf16[128,16,640]{2,0,1:T(8,128)(2,1)} copy(bf16[128,16,640]{2,1,0:T(8,128)(2,1)} %param.7) | data formatting | bytes 5242880 | tf_op args[0]
  4.4 85.1 %shard_map.86 = (bf16[640,2048]{1,0:T(8,128)(2,1)}, f32[8,1024]{1,0:T(8,128)}) custom-call(bf16[16,128,640]{2,1,0:T(8,128)(2,1)} %bitcast.9, bf16[1024,2048]{1,0:T(8,128)(2,1)} %constant.4.clone.table_hbm, bf16[2048,1024]{1,0:T(8,128)(2,1)} %constant.5.clone.back_hbm, f32[21,2,1024]{2,1,0:T(2,128)} %bitcast.11, f32[1,1024]{1,0:T(1,128)} %bitcast.13, ...), custom_call_target="tpu_custom_call" | custom-call | flops 10737418240 | bytes 20000000 | tf_op jit(solution)/shard_map/pallas_call | solution.py:328
  89.5 4.7 %shard_map.87 = (bf16[640,2048]{1,0:T(8,128)(2,1)}, f32[8,1024]{1,0:T(8,128)}) custom-call(bf16[640,2048]{1,0:T(8,128)(2,1)} %get-tuple-element.6.signal_in, f32[8,1024]{1,0:T(8,128)} %get-tuple-element.7.charge_in), custom_call_target="tpu_custom_call" | custom-call | tf_op jit(solution)/shard_map/pallas_call | solution.py:379
